TPU v7x, 32 devices: a whole 2x2x4 slice. The times are simulated.
32 devices in a mesh: lon: 8 (over y, x, core), lat: 4 (over z).
Axes of the slice: x: 2, y: 2, z: 4, core: 2. Of those that a mesh axis runs over, the one named last changes fastest.
Arguments:
- control: float32 [2, 16, 256, 1024], P(None, None, 'lat', 'lon'), may hold values from -6 to 6
- land_mask: int32 [256, 1024], P('lat', 'lon'), may hold values 0 or 1
- std_dev: float32 [2, 16], replicated, may hold values from 0.3 to 3
- innovation: float32 [32, 16, 1024], P(None, 'lat', 'lon'), may hold values from -6 to 6
- inverse_var: float32 [32, 16, 1024], P(None, 'lat', 'lon'), may hold values from 0.25 to 4
- obs_row: int32 [16, 1024], P('lat', 'lon'), may hold values from 0 to 62
- obs_col: int32 [16, 1024], P('lat', 'lon'), may hold values from 0 to 126
- frac_row: float32 [16, 1024], P('lat', 'lon'), may hold values from 0 to 1
- frac_col: float32 [16, 1024], P('lat', 'lon'), may hold values from 0 to 1
- counts: int32 [16, 64], P('lat', 'lon'), may hold values from 0 to 16, as said below
Outputs:
- gradient: float32 [2, 16, 256, 1024], P(None, None, 'lat', 'lon')
Inputs may be any that keep to these rules, and one draw needn't show every extreme that they name: `counts`: each tile gets at most 16 live slots from one holder; in every draw some tile gets exactly 16 from every holder. Dense tiles are drawn from the seed.
All inputs are finite; a program needn't handle non-finite values. No bound on the sum of `land_mask` on one device may be relied on, other than what follows from the above.
Results may differ from a plain program's by a relative error of at most 0.000075.
Values sent between devices are 32-bit elements; how exact they have to be, the bound alone decides.
A program may use at most 64 MiB of HBM per device.

v0:
```python
import functools

import jax
import jax.numpy as jnp
import numpy as np
from jax import lax
from jax.experimental import pallas as pl
from jax.experimental.pallas import tpu as pltpu
from jax.sharding import PartitionSpec as P

HALF = 50
SPREAD = HALF / 2.0
_TAPS = np.exp(-0.5 * (np.arange(-HALF, HALF + 1) / SPREAD) ** 2)
NORM = float(1.0 / np.sqrt(np.sum(_TAPS * _TAPS)))
CHUNK = 128
GROUP = 32
VMEM_LIMIT = 48 * 1024 * 1024
VMEM = pl.BlockSpec(memory_space=pltpu.VMEM)
SMEM = pl.BlockSpec(memory_space=pltpu.SMEM)


def split(x):
    hi = x.astype(jnp.bfloat16)
    lo = (x - hi.astype(jnp.float32)).astype(jnp.bfloat16)
    return hi, lo


def taps(distance):
    values = jnp.exp(distance * distance * (-0.5 / (SPREAD * SPREAD))) * NORM
    return jnp.where(jnp.abs(distance) < HALF + 0.5, values, 0.0)


def iota(shape, dim):
    return lax.broadcasted_iota(jnp.int32, shape, dim).astype(jnp.float32)


def arrange(values, rank, out_ref):
    hi = values.astype(jnp.bfloat16)
    low, least = split(values - hi.astype(jnp.float32))
    parts = jnp.concatenate([hi.astype(jnp.float32), low.astype(jnp.float32), least.astype(jnp.float32)], axis=0)
    parts = parts.astype(jnp.bfloat16)
    count, slots = values.shape
    for k in range(slots // CHUNK):
        place = iota((CHUNK, slots), 0) + float(k * CHUNK)
        one = jnp.where(place == rank, 1.0, 0.0).astype(jnp.bfloat16)
        moved = lax.dot_general(
            parts, one, (((1,), (1,)), ((), ())), preferred_element_type=jnp.float32
        )
        out_ref[:, k * CHUNK : (k + 1) * CHUNK] = (
            moved[:count] + moved[count : 2 * count] + moved[2 * count :]
        )


def meta_kernel(mask_ref, row_ref, col_ref, frow_ref, fcol_ref, counts_ref, out_ref, rank_ref, raw):
    mask = mask_ref[...].astype(jnp.bfloat16)
    height, width = mask.shape
    holders, lanes = row_ref.shape
    tiles = counts_ref.shape[1]
    cap = lanes // tiles
    tile = lax.broadcasted_iota(jnp.int32, (tiles, lanes), 0)
    lane = lax.broadcasted_iota(jnp.int32, (tiles, lanes), 1)
    inside = (lane >= tile * cap) & (lane < tile * cap + cap)
    repeat = jnp.where(inside, 1.0, 0.0).astype(jnp.bfloat16)
    first = jnp.sum(jnp.where(inside, tile * cap, 0).astype(jnp.float32), axis=0, keepdims=True)
    number = iota((1, lanes), 1) - first
    limits = jnp.dot(
        counts_ref[...].astype(jnp.float32).astype(jnp.bfloat16),
        repeat,
        preferred_element_type=jnp.float32,
    )
    for s in range(holders):
        row = row_ref[pl.ds(s, 1), :].astype(jnp.float32)
        col = col_ref[pl.ds(s, 1), :].astype(jnp.float32)
        a = frow_ref[pl.ds(s, 1), :]
        b = fcol_ref[pl.ds(s, 1), :]
        x = iota((width, lanes), 0) - col
        at_left = jnp.where(x == 0.0, 1.0, 0.0).astype(jnp.bfloat16)
        at_right = jnp.where(x == 1.0, 1.0, 0.0).astype(jnp.bfloat16)
        left = jnp.dot(mask, at_left, preferred_element_type=jnp.float32)
        right = jnp.dot(mask, at_right, preferred_element_type=jnp.float32)
        y = iota((height, lanes), 0) - row
        m00 = jnp.sum(jnp.where(y == 0.0, left, 0.0), axis=0, keepdims=True)
        m01 = jnp.sum(jnp.where(y == 0.0, right, 0.0), axis=0, keepdims=True)
        m10 = jnp.sum(jnp.where(y == 1.0, left, 0.0), axis=0, keepdims=True)
        m11 = jnp.sum(jnp.where(y == 1.0, right, 0.0), axis=0, keepdims=True)
        live = jnp.where(number < limits[s : s + 1], 1.0, 0.0)
        at = pl.ds(s * lanes, lanes)
        raw[0:1, at] = row
        raw[1:2, at] = col
        raw[2:3, at] = (1.0 - a) * (1.0 - b) * m00 * live
        raw[3:4, at] = (1.0 - a) * b * m01 * live
        raw[4:5, at] = a * (1.0 - b) * m10 * live
        raw[5:6, at] = a * b * m11 * live
        raw[6:7, at] = live
        raw[7:8, at] = live


    slots = raw.shape[1]
    order = jnp.where(raw[6:7, :] > 0.0, raw[1:2, :], float(width)) * slots + iota((1, slots), 1)
    eye = iota((CHUNK, CHUNK), 0) == iota((CHUNK, CHUNK), 1)
    rank = jnp.zeros((1, slots), jnp.float32)
    for k in range(slots // CHUNK):
        piece = order[:, k * CHUNK : (k + 1) * CHUNK]
        column = jnp.sum(jnp.where(eye, piece, 0.0), axis=1, keepdims=True)
        rank = rank + jnp.sum(jnp.where(column < order, 1.0, 0.0), axis=0, keepdims=True)
    rank_ref[...] = rank
    arrange(raw[...], rank, out_ref)


def neighbours(n_lon, n_lat):
    lon, lat = lax.axis_index("lon"), lax.axis_index("lat")
    found = []
    for t in range(9):
        if t == 4:
            continue
        dp, dq = t // 3 - 1, t % 3 - 1
        there = (lat + dp >= 0) & (lat + dp < n_lat)
        target = {"lon": lax.rem(lon + dq + n_lon, n_lon), "lat": lat + dp}
        found.append((t, there, target, dp))
    return found


def guarded(dp, there, body):
    if dp == 0:
        body()
    else:
        pl.when(there)(body)


def greet(near, between=None):
    barrier = pltpu.get_barrier_semaphore()
    for _, there, target, dp in near:
        guarded(dp, there, lambda target=target: pl.semaphore_signal(barrier, inc=1, device_id=target))
    if between is not None:
        between()
    peers = sum(jnp.where(there, 1, 0) for _, there, _, _ in near)
    pl.semaphore_wait(barrier, peers)


def exchange(near, source, target_ref, send_sem, recv_sem):
    copies = []
    for t, there, target, dp in near:
        copy = pltpu.make_async_remote_copy(
            src_ref=source(t),
            dst_ref=target_ref.at[8 - t],
            send_sem=send_sem.at[t],
            recv_sem=recv_sem.at[8 - t],
            device_id=target,
        )
        guarded(dp, there, copy.start)
        copies.append((t, there, dp, copy))
    return copies


def finish(near, copies, target_ref, recv_sem):
    for t, there, dp, copy in copies:
        guarded(dp, there, copy.wait_send)
    for t, there, target, dp in near:
        arrival = pltpu.make_async_remote_copy(
            src_ref=target_ref.at[t],
            dst_ref=target_ref.at[t],
            send_sem=recv_sem.at[t],
            recv_sem=recv_sem.at[t],
            device_id=target,
        )
        guarded(dp, there, arrival.wait_recv)


def clear_missing(near, ref):
    for t, there, _, dp in near:
        if dp == 0:
            continue

        @pl.when(jnp.logical_not(there))
        def _():
            ref[t] = jnp.zeros(ref.shape[1:], ref.dtype)


def share_kernel(n_lon, n_lat, *refs):
    inputs, (meta_ref, rank_ref, out_ref, used_ref, raw, send_sem, recv_sem) = refs[:6], refs[6:]
    height, width = inputs[0].shape
    near = neighbours(n_lon, n_lat)
    greet(near, lambda: meta_kernel(*inputs, meta_ref, rank_ref, raw))
    copies = exchange(near, lambda t: meta_ref, out_ref, send_sem, recv_sem)
    out_ref[4] = meta_ref[...]
    clear_missing(near, out_ref)
    finish(near, copies, out_ref, recv_sem)
    slots = out_ref.shape[2]
    for t in range(9):
        meta = out_ref[t]
        y, x = meta[0:1] + float((t // 3 - 1) * height), meta[1:2] + float((t % 3 - 1) * width)
        reached = (
            (y >= -(HALF + 1.0)) & (y <= height - 1.0 + HALF)
            & (x >= -(HALF + 1.0)) & (x <= width - 1.0 + HALF)
        )
        live = jnp.where(reached, meta[6:7], 0.0)
        for c in range(slots // CHUNK):
            used_ref[t : t + 1, c : c + 1] = jnp.max(
                live[:, c * CHUNK : (c + 1) * CHUNK], axis=1, keepdims=True
            )


def misfit_kernel(
    n_lon, n_lat, part_ref, owned_ref, meta_ref, rank_ref, std_ref, out_ref,
    landed, mine, placed, send_sem, recv_sem, send_sem_2, recv_sem_2,
):
    near = neighbours(n_lon, n_lat)
    greet(near)
    copies = exchange(near, lambda t: part_ref.at[t], landed, send_sem, recv_sem)
    clear_missing(near, landed)
    clear_missing(near, out_ref)
    arrange(owned_ref[...], rank_ref[...], placed)
    finish(near, copies, landed, recv_sem)
    total = part_ref[4]
    for t in range(9):
        if t != 4:
            total = total + landed[t]
    rows = total.shape[0]
    scale = std_ref[...]
    live = meta_ref[6:7, :]
    mine[...] = scale * placed[rows:, :] * (scale * total - placed[:rows, :]) * live
    out_ref[4] = mine[...]
    copies = exchange(near, lambda t: mine, out_ref, send_sem_2, recv_sem_2)
    finish(near, copies, out_ref, recv_sem_2)


def tables(meta, shift_y, shift_x, height, width, first):
    chunk = meta.shape[1]
    y = meta[0:1] + shift_y - iota((height, chunk), 0)
    x = meta[1:2] + shift_x - first - iota((width, chunk), 0)
    left, right = taps(x), taps(x + 1.0)
    along_x = [
        meta[2:3] * left + meta[3:4] * right,
        meta[4:5] * left + meta[5:6] * right,
    ]
    return [taps(y), taps(y + 1.0)], along_x


def walk(meta_ref, used_ref, height, width, work, skip=None):
    chunks = meta_ref.shape[2] // CHUNK
    near_cols = width // 2 if HALF <= width // 2 else width
    for dq in (-1, 0, 1):
        cols = near_cols if dq else width
        first = width - cols if dq > 0 else 0

        @pl.loop(0, 3 * chunks)
        def _(step):
            p, c = lax.div(step, chunks), lax.rem(step, chunks)
            t = 3 * p + (dq + 1)
            at = pl.ds(pl.multiple_of(c * CHUNK, CHUNK), CHUNK)
            meta = meta_ref[t, :, at]
            shift_y = (p - 1).astype(jnp.float32) * height
            shift_x = float(dq * width)
            used = used_ref[t, c] > 0.5

            @pl.when(used)
            def _():
                along_y, along_x = tables(meta, shift_y, shift_x, height, cols, first)
                work(dq, first, cols, t, at, along_y, along_x)

            if skip is not None:

                @pl.when(jnp.logical_not(used))
                def _():
                    skip(t, at)


def forward_kernel(meta_ref, used_ref, control_ref, mask_ref, out_ref, own, side, ys, xs):
    levels, height, width = control_ref.shape
    half = side.shape[2] // 3
    mask = mask_ref[...].astype(jnp.float32)

    @pl.loop(0, levels, unroll=8)
    def _(l):
        field = control_ref[l] * mask
        hi, lo = split(field)
        at = pl.ds(pl.multiple_of(l * height, height), height)
        own[at, 0:width] = hi
        own[at, width : 2 * width] = hi
        own[at, 2 * width : 3 * width] = lo
        hi = hi.astype(jnp.float32)
        lo = field - hi
        for k, first in enumerate((0, width - half)):
            h, low = hi[:, first : first + half], lo[:, first : first + half]
            side[k, at, :] = jnp.concatenate([h, h, low], axis=1).astype(jnp.bfloat16)

    rows = GROUP * height

    def work(dq, first, cols, t, where, along_y, along_x):
        for i in range(2):
            lanes = slice(i * CHUNK, (i + 1) * CHUNK)
            ys[:, lanes] = along_y[i]
            hi, lo = split(along_x[i])
            xs[0:cols, lanes] = hi
            xs[cols : 2 * cols, lanes] = lo
            xs[2 * cols : 3 * cols, lanes] = hi

        @pl.loop(0, levels // GROUP)
        def _(g):
            at = pl.ds(pl.multiple_of(g * rows, rows), rows)
            left = own[at, :] if dq == 0 else side[(dq + 1) // 2, at, :]
            wide = jnp.dot(left, xs[0 : 3 * cols], preferred_element_type=jnp.float32)
            total = jnp.sum(wide.reshape(GROUP, height, -1) * ys[...][None], axis=1)
            total = total[:, :CHUNK] + total[:, CHUNK:]
            out_ref[t, pl.ds(pl.multiple_of(g * GROUP, GROUP), GROUP), where] = total

    def skip(t, where):
        out_ref[t, :, where] = jnp.zeros((levels, CHUNK), jnp.float32)

    walk(meta_ref, used_ref, height, width, work, skip)


def backward_kernel(meta_ref, used_ref, v_ref, control_ref, mask_ref, out_ref, ys, xs):
    levels, height, width = control_ref.shape
    out_ref[...] = jnp.zeros_like(out_ref)
    contract = (((1,), (1,)), ((), ()))

    def work(dq, first, cols, t, where, along_y, along_x):
        if cols < width:
            blank = jnp.zeros((width - cols, CHUNK), jnp.float32)
            order = (lambda x: [x, blank]) if first == 0 else (lambda x: [blank, x])
            along_x = [jnp.concatenate(order(x), axis=0) for x in along_x]
        for i in range(2):
            lanes = slice(i * CHUNK, (i + 1) * CHUNK)
            ys[i] = along_y[i]
            hi, lo = split(along_x[i])
            xs[0:width, lanes] = hi
            xs[width : 2 * width, lanes] = lo

        @pl.loop(0, levels // GROUP)
        def _(g):
            at = pl.ds(pl.multiple_of(g * GROUP, GROUP), GROUP)
            v = v_ref[t, at, where]
            his, los = [], []
            for i in range(2):
                b = (v[:, None, :] * ys[i][None]).reshape(GROUP * height, CHUNK)
                hi, lo = split(b)
                his.append(hi)
                los.append(lo)
            wide = lax.dot_general(
                jnp.concatenate(his, axis=1), xs[...], contract, preferred_element_type=jnp.float32
            )
            rest = lax.dot_general(
                jnp.concatenate(los, axis=1), xs[0:width, :], contract, preferred_element_type=jnp.float32
            )
            total = wide[:, :width] + wide[:, width:] + rest
            out_ref[at] += total.reshape(GROUP, height, width)

    walk(meta_ref, used_ref, height, width, work)
    mask = mask_ref[...].astype(jnp.float32)

    @pl.loop(0, levels, unroll=8)
    def _(l):
        out_ref[l] = control_ref[l] + mask * out_ref[l]


def to_owner(values, n_lat, n_lon):
    count, cap = values.shape[0], values.shape[2] // n_lon
    blocks = values.reshape(count, n_lat, n_lon, cap).transpose(1, 2, 0, 3)
    blocks = blocks.reshape(n_lat * n_lon, count * cap)
    moved = lax.all_to_all(blocks, ("lat", "lon"), split_axis=0, concat_axis=0, tiled=True)
    return moved.reshape(n_lat * n_lon, count, cap).transpose(1, 0, 2).reshape(count, -1)


def shards(
    n_lon, n_lat, control, land_mask, std_dev, innovation, inverse_var,
    obs_row, obs_col, frac_row, frac_col, counts,
):
    levels = control.shape[0] * control.shape[1]
    height, width = control.shape[2:]
    slots = obs_row.shape[0] * obs_row.shape[1]
    fields = control.reshape(levels, height, width)
    scales = std_dev.reshape(levels, 1)
    f32 = jnp.float32
    params = functools.partial(pltpu.CompilerParams, vmem_limit_bytes=VMEM_LIMIT)
    sems = pltpu.SemaphoreType.DMA((9,))

    meta, rank, meta_all, used = pl.pallas_call(
        functools.partial(share_kernel, n_lon, n_lat),
        out_shape=[
            jax.ShapeDtypeStruct((8, slots), f32),
            jax.ShapeDtypeStruct((1, slots), f32),
            jax.ShapeDtypeStruct((9, 8, slots), f32),
            jax.ShapeDtypeStruct((9, slots // CHUNK), f32),
        ],
        in_specs=[VMEM] * 6,
        out_specs=[VMEM] * 4,
        scratch_shapes=[pltpu.VMEM((8, slots), f32), sems, sems],
        compiler_params=params(collective_id=0, has_side_effects=True),
        name="share_slots",
    )(land_mask, obs_row, obs_col, frac_row, frac_col, counts)

    owned = to_owner(jnp.concatenate([innovation, inverse_var], axis=0), n_lat, n_lon)

    half = width // 2 if HALF <= width // 2 else width
    parts = pl.pallas_call(
        forward_kernel,
        out_shape=jax.ShapeDtypeStruct((9, levels, slots), f32),
        in_specs=[VMEM, SMEM, VMEM, VMEM],
        out_specs=VMEM,
        scratch_shapes=[
            pltpu.VMEM((levels * height, 3 * width), jnp.bfloat16),
            pltpu.VMEM((2, levels * height, 3 * half), jnp.bfloat16),
            pltpu.VMEM((height, 2 * CHUNK), f32),
            pltpu.VMEM((3 * width, 2 * CHUNK), jnp.bfloat16),
        ],
        compiler_params=params(),
        name="partial_columns",
    )(meta_all, used, fields, land_mask)

    scaled = pl.pallas_call(
        functools.partial(misfit_kernel, n_lon, n_lat),
        out_shape=jax.ShapeDtypeStruct((9, levels, slots), f32),
        in_specs=[VMEM] * 5,
        out_specs=VMEM,
        scratch_shapes=[
            pltpu.VMEM((9, levels, slots), f32),
            pltpu.VMEM((levels, slots), f32),
            pltpu.VMEM((2 * levels, slots), f32),
            sems, sems, sems, sems,
        ],
        compiler_params=params(collective_id=1, has_side_effects=True),
        name="misfits",
    )(parts, owned, meta, rank, scales)

    gradient = pl.pallas_call(
        backward_kernel,
        out_shape=jax.ShapeDtypeStruct((levels, height, width), f32),
        in_specs=[VMEM, SMEM, VMEM, VMEM, VMEM],
        out_specs=VMEM,
        scratch_shapes=[
            pltpu.VMEM((2, height, CHUNK), f32),
            pltpu.VMEM((2 * width, 2 * CHUNK), jnp.bfloat16),
        ],
        compiler_params=params(),
        name="gradient",
    )(meta_all, used, scaled, fields, land_mask)
    return gradient.reshape(control.shape)


def solution(mesh):
    tile = P("lat", "lon")
    in_specs = (
        P(None, None, "lat", "lon"), tile, P(),
        P(None, "lat", "lon"), P(None, "lat", "lon"),
        tile, tile, tile, tile, tile,
    )
    body = functools.partial(shards, mesh.shape["lon"], mesh.shape["lat"])
    return jax.shard_map(
        body, mesh=mesh, in_specs=in_specs,
        out_specs=P(None, None, "lat", "lon"), check_vma=False,
    )
```

profile of v0, /device:TPU:8, one launch (start us, length us, event | category | flops | bytes accessed | tf_op | source)
XLA Modules:
  0.0 59.1 jit_solution(5659659878049102608)
XLA Ops:
  0.0 0.0 copy-start.7
  0.0 1.0 %copy.19 = f32[32,4,128]{0,2,1:T(8,128)S(1)} copy(f32[32,4,128]{2,1,0:T(4,128)} %param.13) | data formatting | bytes 131072 | tf_op args[3]
  1.0 0.0 copy-done.7
  1.0 0.1 copy.20
  1.1 0.1 pad_maximum_fusion
  1.3 0.3 copy.21
  1.6 0.0 copy-start
  1.7 1.0 %all_to_all.8 = f32[32,1,1024]{2,1,0:T(1,128)} reshape(f32[4,8,64,16]{3,2,1,0:T(8,128)S(1)} %copy.21) | data formatting | bytes 262144 | tf_op jit(solution)/shard_map/all_to_all | solution.py:361
  2.7 0.0 copy-start.8
  2.7 0.0 copy-start.1
  2.7 6.0 %all-to-all-start = ((f32[32,1,1024]{2,1,0:T(1,128)}), f32[32,1,1024]{2,1,0:T(1,128)S(1)}, u32[]{:S(2)}, u32[]{:S(2)}) async-start(f32[32,1,1024]{2,1,0:T(1,128)} %all_to_all.8), calls=%async_computation | async-start | bytes 262144 | tf_op jit(solution)/shard_map/all_to_all | solution.py:361
  8.8 0.0 copy-done.8
  8.8 0.0 copy-start.2
  8.8 0.0 copy-start.3
  8.8 0.0 copy-start.4
  8.8 0.0 copy-start.5
  8.8 0.0 copy-start.6
  8.8 0.1 reshape.29.std_ref
  8.9 0.0 copy-done.1
  8.9 0.5 copy-done.2
  9.5 0.0 copy-done.3
  9.5 0.0 copy-done.4
  9.5 0.0 copy-done.5
  9.5 0.0 copy-done.6
  9.5 7.6 %share_slots.1 = (f32[8,512]{1,0:T(8,128)S(1)}, f32[1,512]{1,0:T(1,128)S(1)}, f32[9,8,512]{2,1,0:T(8,128)S(1)}, f32[9,4]{1,0:T(8,128)S(1)}) custom-call(s32[64,128]{1,0:T(8,128)S(1)} %copy-done.1, s32[4,128]{1,0:T(4,128)S(1)} %copy-done.2, s32[4,128]{1,0:T(4,128)S(1)} %copy-done.3, f32[4,128]{1,0:T(4,128)S(1)} %copy-done.4, f32[4,128]{1,0:T(4,128)S(1)} %copy-done.5, ...), custom_call_target="tpu_custom_call" | custom-call | tf_op jit(solution)/shard_map/share_slots/pallas_call | solution.py:378
  17.1 0.0 copy-done
  17.2 11.3 %partial_columns.1.part_ref = f32[9,32,512]{2,1,0:T(8,128)S(1)} custom-call(f32[9,8,512]{2,1,0:T(8,128)S(1)} %get-tuple-element.9.meta_ref, f32[9,4]{1,0:T(8,128)S(1)} %get-tuple-element.10.used_ref, f32[32,64,128]{2,1,0:T(8,128)S(1)} %bitcast.11, s32[64,128]{1,0:T(8,128)S(1)} %copy-done.1), custom_call_target="tpu_custom_call" | custom-call | tf_op jit(solution)/shard_map/partial_columns/pallas_call | solution.py:396
  28.4 0.0 all-to-all-done
  28.5 0.2 copy.23
  28.7 0.3 copy.24
  29.0 0.1 copy.25.owned_ref
  29.1 16.1 %misfits.1.v_ref = f32[9,32,512]{2,1,0:T(8,128)S(1)} custom-call(f32[9,32,512]{2,1,0:T(8,128)S(1)} %partial_columns.1.part_ref, f32[64,512]{1,0:T(8,128)S(1)} %copy.25.owned_ref, f32[8,512]{1,0:T(8,128)S(1)} %get-tuple-element.11.meta_ref, f32[1,512]{1,0:T(1,128)S(1)} %get-tuple-element.12.rank_ref, f32[32,1]{1,0:T(8,128)S(1)} %reshape.29.std_ref), custom_call_target="tpu_custom_call" | custom-call | tf_op jit(solution)/shard_map/misfits/pallas_call | solution.py:411
  45.3 13.8 %gradient.1 = f32[32,64,128]{2,1,0:T(8,128)} custom-call(f32[9,8,512]{2,1,0:T(8,128)S(1)} %get-tuple-element.9.meta_ref, f32[9,4]{1,0:T(8,128)S(1)} %get-tuple-element.10.used_ref, f32[9,32,512]{2,1,0:T(8,128)S(1)} %misfits.1.v_ref, f32[32,64,128]{2,1,0:T(8,128)S(1)} %bitcast.12, s32[64,128]{1,0:T(8,128)S(1)} %copy-done.1), custom_call_target="tpu_custom_call" | custom-call | tf_op jit(solution)/shard_map/gradient/pallas_call | solution.py:426
Async XLA Ops:
  0.0 1.0 %copy-start.7 = (f32[32,4,128]{2,1,0:T(4,128)S(1)}, f32[32,4,128]{2,1,0:T(4,128)}, u32[]{:S(2)}) copy-start(f32[32,4,128]{2,1,0:T(4,128)} %param.14) | copy-start | bytes 196612
  1.6 15.5 %copy-start = (f32[2,16,64,128]{3,2,1,0:T(8,128)S(1)}, f32[2,16,64,128]{3,2,1,0:T(8,128)}, u32[]{:S(2)}) copy-start(f32[2,16,64,128]{3,2,1,0:T(8,128)} %param.10) | copy-start | bytes 3145732
  2.7 6.1 %copy-start.8 = (f32[2,16]{1,0:T(2,128)S(1)}, f32[2,16]{1,0:T(2,128)}, u32[]{:S(2)}) copy-start(f32[2,16]{1,0:T(2,128)} %param.12) | copy-start | bytes 388
  2.7 6.2 %copy-start.1 = (s32[64,128]{1,0:T(8,128)S(1)}, s32[64,128]{1,0:T(8,128)}, u32[]{:S(2)}) copy-start(s32[64,128]{1,0:T(8,128)} %mask_ref.3) | copy-start | bytes 98308
  2.7 25.7 %all-to-all-start = ((f32[32,1,1024]{2,1,0:T(1,128)}), f32[32,1,1024]{2,1,0:T(1,128)S(1)}, u32[]{:S(2)}, u32[]{:S(2)}) async-start(f32[32,1,1024]{2,1,0:T(1,128)} %all_to_all.8), calls=%async_computation | async-start | bytes 262144 | tf_op jit(solution)/shard_map/all_to_all | solution.py:361
  8.8 0.7 %copy-start.2 = (s32[4,128]{1,0:T(4,128)S(1)}, s32[4,128]{1,0:T(4,128)}, u32[]{:S(2)}) copy-start(s32[4,128]{1,0:T(4,128)} %refs_1_.1) | copy-start | bytes 6148
  8.8 0.7 %copy-start.3 = (s32[4,128]{1,0:T(4,128)S(1)}, s32[4,128]{1,0:T(4,128)}, u32[]{:S(2)}) copy-start(s32[4,128]{1,0:T(4,128)} %refs_2_.1) | copy-start | bytes 6148
  8.8 0.7 %copy-start.4 = (f32[4,128]{1,0:T(4,128)S(1)}, f32[4,128]{1,0:T(4,128)}, u32[]{:S(2)}) copy-start(f32[4,128]{1,0:T(4,128)} %refs_3_.1) | copy-start | bytes 6148
  8.8 0.7 %copy-start.5 = (f32[4,128]{1,0:T(4,128)S(1)}, f32[4,128]{1,0:T(4,128)}, u32[]{:S(2)}) copy-start(f32[4,128]{1,0:T(4,128)} %refs_4_.1) | copy-start | bytes 6148
  8.8 0.7 %copy-start.6 = (s32[4,8]{1,0:T(4,128)S(1)}, s32[4,8]{1,0:T(4,128)}, u32[]{:S(2)}) copy-start(s32[4,8]{1,0:T(4,128)} %refs_5_.1) | copy-start | bytes 388
where the time goes:
time: 59.9 us; the launch traced here: 59.1 us
  Pallas kernels  48.9 us (82%)
  starting transfers between devices  6.04 us (10%)
  local copies, waits for them, and re-layouts  3.87 us (6%)
    pallas_call x1, Pallas kernels, shards(): pl.pallas_call(functools.partial(misfit_kernel, n_lon, n_lat), out_shape=...  16.1 us
    pallas_call x1, Pallas kernels, shards(): pl.pallas_call(backward_kernel, out_shape=jax.ShapeDtypeStruct((levels, h...  13.8 us
    pallas_call x1, Pallas kernels, shards(): pl.pallas_call(forward_kernel, out_shape=jax.ShapeDtypeStruct((9, levels,...  11.3 us
    pallas_call x1, Pallas kernels, shards(): pl.pallas_call(functools.partial(share_kernel, n_lon, n_lat), out_shape=[...  7.61 us
    all_to_all x1, starting transfers between devices, to_owner(): lax.all_to_all(blocks, ('lat', 'lon'), split_axis=0, concat_axis=0, tiled...  6.04 us
    unnamed x20, local copies, waits for them, and re-layouts  1.75 us
    all_to_all x2, local copies, waits for them, and re-layouts, to_owner(): lax.all_to_all(blocks, ('lat', 'lon'), split_axis=0, concat_axis=0, tiled...  1.25 us
  transfers between devices with their start and end apart: 1, of which 0 were waited for; matrix products, arithmetic and copies ran while one was open for 0% of the time, Pallas kernels for 32%

commit v1 on v0

v1 whole, which is shorter than its diff:
```python
import functools

import jax
import jax.numpy as jnp
import numpy as np
from jax import lax
from jax.experimental import pallas as pl
from jax.experimental.pallas import tpu as pltpu
from jax.sharding import PartitionSpec as P

HALF = 50
SPREAD = HALF / 2.0
_TAPS = np.exp(-0.5 * (np.arange(-HALF, HALF + 1) / SPREAD) ** 2)
NORM = float(1.0 / np.sqrt(np.sum(_TAPS * _TAPS)))
CHUNK = 128
GROUPS = 4
PIECE = HALF // 2
VMEM_LIMIT = 56 * 1024 * 1024
VMEM = pl.BlockSpec(memory_space=pltpu.VMEM)
F32, BF16 = jnp.float32, jnp.bfloat16


def split(x):
    hi = x.astype(BF16)
    return hi, (x - hi.astype(F32)).astype(BF16)


def taps(distance):
    values = jnp.exp(distance * distance * (-0.5 / (SPREAD * SPREAD))) * NORM
    return jnp.where(jnp.abs(distance) < HALF + 0.5, values, 0.0)


def iota(shape, dim):
    return lax.broadcasted_iota(jnp.int32, shape, dim).astype(F32)


def dot(a, b):
    return jnp.dot(a, b, preferred_element_type=F32)


def roll(x, shift):
    shift = shift % x.shape[1]
    return pltpu.roll(x, shift, 1) if shift else x


def packing(rows):
    per = 128 // PIECE
    packed = -(-2 * rows // (8 * per)) * 8
    segments, at = [], 0
    while at < 2 * rows:
        half, row = at // rows, at % rows
        slot, place = at // packed, at % packed
        count = min(rows - row, packed - place)
        segments.append((half, row, count, slot, place))
        at += count
    return packed, segments


def pack(x, first):
    rows, width = x.shape
    packed, segments = packing(rows)
    lane = lax.broadcasted_iota(jnp.int32, (packed, width), 1)
    result = None
    for slot in range(segments[-1][3] + 1):
        mine = [s for s in segments if s[3] == slot]
        pieces = [
            roll(x[row : row + count], slot * PIECE - (first + half * PIECE))
            for half, row, count, _, _ in mine
        ]
        lacking = packed - sum(s[2] for s in mine)
        if lacking:
            pieces.append(x[:lacking])
        piece = jnp.concatenate(pieces, axis=0) if len(pieces) > 1 else pieces[0]
        result = piece if result is None else jnp.where(lane >= slot * PIECE, piece, result)
    return result


def unpack(left, right, rows):
    _, segments = packing(rows)
    lane = lax.broadcasted_iota(jnp.int32, (rows, left.shape[1]), 1)
    result = None
    for k, source in enumerate((left, right)):
        for half in range(2):
            target = k * HALF + half * PIECE
            pieces = [
                roll(source[place : place + count], target - slot * PIECE)
                for h, _, count, slot, place in segments
                if h == half
            ]
            piece = jnp.concatenate(pieces, axis=0)
            result = piece if result is None else jnp.where(lane >= target, piece, result)
    return result


def swap_blocks(blocks):
    count = len(blocks)
    width = blocks[0].shape[1] // count
    group = lax.broadcasted_iota(jnp.int32, blocks[0].shape, 1) // width
    bit = 1
    while bit < count:
        low = (group & bit) == 0
        fresh = []
        for k in range(count):
            other = blocks[k ^ bit]
            if k & bit == 0:
                fresh.append(jnp.where(low, blocks[k], roll(other, width * bit)))
            else:
                fresh.append(jnp.where(low, roll(other, -width * bit), blocks[k]))
        blocks = fresh
        bit *= 2
    return blocks


def describe(mask_ref, row_ref, col_ref, frow_ref, fcol_ref, counts_ref, out_ref):
    mask = mask_ref[...].astype(BF16)
    height, width = mask.shape
    holders, lanes = row_ref.shape
    tiles = counts_ref.shape[1]
    cap = lanes // tiles
    tile = lax.broadcasted_iota(jnp.int32, (tiles, lanes), 0)
    lane = lax.broadcasted_iota(jnp.int32, (tiles, lanes), 1)
    inside = (lane >= tile * cap) & (lane < tile * cap + cap)
    repeat = jnp.where(inside, 1.0, 0.0).astype(BF16)
    first = jnp.sum(jnp.where(inside, tile * cap, 0).astype(F32), axis=0, keepdims=True)
    number = iota((1, lanes), 1) - first
    limits = dot(counts_ref[...].astype(F32).astype(BF16), repeat)
    for s in range(holders):
        row = row_ref[pl.ds(s, 1), :].astype(F32)
        col = col_ref[pl.ds(s, 1), :].astype(F32)
        a = frow_ref[pl.ds(s, 1), :]
        b = fcol_ref[pl.ds(s, 1), :]
        x = iota((width, lanes), 0) - col
        both = jnp.concatenate(
            [jnp.where(x == 0.0, 1.0, 0.0).astype(BF16), jnp.where(x == 1.0, 1.0, 0.0).astype(BF16)], axis=1
        )
        found = dot(mask, both)
        left, right = found[:, :lanes], found[:, lanes:]
        y = iota((height, lanes), 0) - row
        m00 = jnp.sum(jnp.where(y == 0.0, left, 0.0), axis=0, keepdims=True)
        m01 = jnp.sum(jnp.where(y == 0.0, right, 0.0), axis=0, keepdims=True)
        m10 = jnp.sum(jnp.where(y == 1.0, left, 0.0), axis=0, keepdims=True)
        m11 = jnp.sum(jnp.where(y == 1.0, right, 0.0), axis=0, keepdims=True)
        live = jnp.where(number < limits[s : s + 1], 1.0, 0.0)
        at = pl.ds(s * lanes, lanes)
        out_ref[0:1, at] = row
        out_ref[1:2, at] = col
        out_ref[2:3, at] = (1.0 - a) * (1.0 - b) * m00 * live
        out_ref[3:4, at] = (1.0 - a) * b * m01 * live
        out_ref[4:5, at] = a * (1.0 - b) * m10 * live
        out_ref[5:6, at] = a * b * m11 * live
        out_ref[6:7, at] = live
        out_ref[7:8, at] = live


def kernel(
    n_lon, n_lat,
    control_ref, mask_ref, std_ref, innov_ref, ivar_ref, row_ref, col_ref, frow_ref, fcol_ref, counts_ref,
    out_ref,
    filt, halo_out, halo_in, back_out, back_in, ahl, grown, field,
    meta, onehot, weight, ytap, ylast, spreadw,
    parts, parts_in, v,
    stage, land_a, turned, land_b, owned,
    halo_ss, halo_rs, back_ss, back_rs, meta_ss, meta_rs, part_ss, part_rs, v_ss, v_rs,
    a_ss, a_rs, b_ss, b_rs,
):
    levels, height, width = control_ref.shape
    slots = meta.shape[2]
    chunks, pairs = slots // CHUNK, slots // (2 * CHUNK)
    size = levels // GROUPS
    rows = size * height
    lon, lat = lax.axis_index("lon"), lax.axis_index("lat")
    sides = [{"lon": lax.rem(lon + n_lon - 1, n_lon), "lat": lat}, {"lon": lax.rem(lon + 1, n_lon), "lat": lat}]
    ends = [({"lon": lon, "lat": lat - 1}, lat > 0), ({"lon": lon, "lat": lat + 1}, lat < n_lat - 1)]

    barrier = pltpu.get_barrier_semaphore()

    @pl.loop(1, n_lon)
    def _(d):
        pl.semaphore_signal(barrier, inc=1, device_id={"lon": lax.rem(lon + d, n_lon), "lat": lat})

    @pl.loop(1, n_lat)
    def _(d):
        pl.semaphore_signal(barrier, inc=1, device_id={"lon": lon, "lat": lax.rem(lat + d, n_lat)})

    mask = mask_ref[...].astype(F32)

    def masked(g):
        part = control_ref[g * size : (g + 1) * size] * mask[None]
        return part.reshape(rows, width)

    def side_copy(out, landed, ss, rs, g, d):
        return pltpu.make_async_remote_copy(
            src_ref=out.at[d, g], dst_ref=landed.at[1 - d, g],
            send_sem=ss.at[d, g], recv_sem=rs.at[1 - d, g], device_id=sides[d],
        )

    def side_wait(out, landed, ss, rs, g):
        for d in range(2):
            pltpu.make_async_remote_copy(
                src_ref=out.at[d, g], dst_ref=landed.at[d, g],
                send_sem=ss.at[d, g], recv_sem=rs.at[d, g], device_id=sides[d],
            ).wait_recv()

    def pack_sides(x, out, g):
        out[0, g] = pack(x, 0)
        out[1, g] = pack(x, width - HALF)

    def halo_pack(g):
        pack_sides(masked(g), halo_out, g)

    def halo_send(g):
        for d in range(2):
            side_copy(halo_out, halo_in, halo_ss, halo_rs, g, d).start()

    halo_pack(0)
    for p in range(n_lat):
        stage[p, 0:levels] = innov_ref[:, p, :]
        stage[p, levels : 2 * levels] = ivar_ref[:, p, :]
    pl.semaphore_wait(barrier, n_lon - 1 + n_lat - 1)
    halo_send(0)

    def first_copy(d):
        return pltpu.make_async_remote_copy(
            src_ref=stage.at[lax.rem(lat + d, n_lat)], dst_ref=land_a.at[lat],
            send_sem=a_ss.at[d], recv_sem=a_rs.at[d],
            device_id={"lon": lon, "lat": lax.rem(lat + d, n_lat)},
        )

    def first_wait(d):
        source = lax.rem(lat + n_lat - d, n_lat)
        pltpu.make_async_remote_copy(
            src_ref=stage.at[source], dst_ref=land_a.at[source],
            send_sem=a_ss.at[d], recv_sem=a_rs.at[d],
            device_id={"lon": lon, "lat": source},
        ).wait_recv()

    @pl.loop(1, n_lat)
    def _(d):
        first_copy(d).start()

    land_a[pl.ds(lat, 1)] = stage[pl.ds(lat, 1)]

    describe(mask_ref, row_ref, col_ref, frow_ref, fcol_ref, counts_ref, meta.at[1])

    def end_copy(src, dst, send_sem, recv_sem, d):
        return pltpu.make_async_remote_copy(
            src_ref=src, dst_ref=dst, send_sem=send_sem, recv_sem=recv_sem, device_id=ends[d][0]
        )

    def at_ends(body):
        for d in range(2):
            pl.when(ends[d][1])(functools.partial(body, d))

    def meta_copy(d):
        return end_copy(meta.at[1], meta.at[2 * (1 - d)], meta_ss.at[d], meta_rs.at[1 - d], d)

    at_ends(lambda d: meta_copy(d).start())
    for g in range(1, GROUPS):
        halo_pack(g)
        halo_send(g)

    for d in range(2):

        @pl.when(jnp.logical_not(ends[d][1]))
        def _():
            meta[2 * d] = jnp.zeros(meta.shape[1:], F32)
            v[2 * d] = jnp.zeros(v.shape[1:], F32)
            parts_in[d] = jnp.zeros(parts_in.shape[1:], F32)

    k = iota((2 * width, width), 0)
    place = jnp.where(k < width, k, jnp.where(k < width + HALF, k - (width + HALF), k - HALF))
    place = jnp.where(k < width + 2 * HALF, place, 1000.0)
    ghi, glo = split(taps(place - iota((2 * width, width), 1)))
    filt[:, 0:width] = ghi
    filt[:, width : 2 * width] = glo

    def tables(t):
        shift = float((t - 1) * height)

        @pl.loop(0, chunks)
        def _(c):
            at = pl.ds(pl.multiple_of(c * CHUNK, CHUNK), CHUNK)
            m = meta[t, :, at]
            y = m[0:1] + shift - iota((height, CHUNK), 0)
            near, far = taps(y), taps(y + 1.0)
            weight[t, c, :, 0:CHUNK] = m[2:3] * near + m[4:5] * far
            weight[t, c, :, CHUNK : 2 * CHUNK] = m[3:4] * near + m[5:6] * far
            ytap[t, :, at] = near
            ylast[t, :, at] = taps(m[0:1] + (shift + 1.0) + 0.0 * iota((8, CHUNK), 0))
            x = iota((width, CHUNK), 0) - m[1:2]
            onehot[t, c, :, 0:CHUNK] = jnp.where(x == 0.0, 1.0, 0.0).astype(BF16)
            onehot[t, c, :, CHUNK : 2 * CHUNK] = jnp.where(x == 1.0, 1.0, 0.0).astype(BF16)
            turn = jnp.transpose(m)
            x = iota((CHUNK, width), 1) - turn[:, 1:2]
            w = jnp.concatenate(
                [
                    jnp.where(x == 0.0, turn[:, 2 + 2 * i : 3 + 2 * i], 0.0)
                    + jnp.where(x == 1.0, turn[:, 3 + 2 * i : 4 + 2 * i], 0.0)
                    for i in range(2)
                ],
                axis=1,
            )
            hi, lo = split(w)
            spreadw[t, 0, at, :] = hi
            spreadw[t, 1, at, :] = lo

    tables(1)

    @pl.loop(1, n_lat)
    def _(d):
        first_wait(d)

    deep = 2 * levels // n_lon
    blocks = [land_a[:, i * deep : (i + 1) * deep, :].reshape(n_lat * deep, width) for i in range(n_lon)]
    for q, block in enumerate(swap_blocks(blocks)):
        turned[q] = block

    def second_copy(d):
        return pltpu.make_async_remote_copy(
            src_ref=turned.at[lax.rem(lon + d, n_lon)], dst_ref=land_b.at[lon],
            send_sem=b_ss.at[d], recv_sem=b_rs.at[d],
            device_id={"lon": lax.rem(lon + d, n_lon), "lat": lat},
        )

    def second_wait(d):
        source = lax.rem(lon + n_lon - d, n_lon)
        pltpu.make_async_remote_copy(
            src_ref=turned.at[source], dst_ref=land_b.at[source],
            send_sem=b_ss.at[d], recv_sem=b_rs.at[d],
            device_id={"lon": source, "lat": lat},
        ).wait_recv()

    @pl.loop(1, n_lon)
    def _(d):
        second_copy(d).start()

    land_b[pl.ds(lon, 1)] = turned[pl.ds(lon, 1)]

    for d in range(2):

        @pl.when(ends[d][1])
        def _(d=d):
            end_copy(meta.at[1], meta.at[2 * d], meta_ss.at[d], meta_rs.at[d], d).wait_recv()

        tables(2 * d)

    def take_observations():
        @pl.loop(1, n_lon)
        def _(d):
            second_wait(d)

        for i, block in enumerate(swap_blocks([land_b[t] for t in range(n_lon)])):
            for s in range(n_lat):
                owned[i * deep : (i + 1) * deep, s * width : (s + 1) * width] = block[s * deep : (s + 1) * deep]

    def smooth(x, beyond):
        hi, lo = split(jnp.concatenate([x, beyond], axis=1))
        wide = dot(hi, filt[...])
        return wide[:, :width] + wide[:, width:] + dot(lo, filt[:, 0:width])

    def part_copy(g, d):
        return end_copy(parts.at[2 * d, g], parts_in.at[1 - d, g], part_ss.at[d, g], part_rs.at[1 - d, g], d)

    def forward(g):
        side_wait(halo_out, halo_in, halo_ss, halo_rs, g)
        hi, lo = split(smooth(masked(g), unpack(halo_in[0, g], halo_in[1, g], rows)))
        ahl[:, 0:width] = hi
        ahl[:, width : 2 * width] = lo
        for t in (0, 2, 1):

            @pl.loop(0, chunks)
            def _(c):
                one = onehot[t, c]
                wide = dot(ahl[...], jnp.concatenate([one, one], axis=0))
                total = jnp.sum(wide.reshape(size, height, 2 * CHUNK) * weight[t, c][None], axis=1)
                at = pl.ds(pl.multiple_of(c * CHUNK, CHUNK), CHUNK)
                parts[t, g, :, at] = total[:, :CHUNK] + total[:, CHUNK:]

            if t == 2:
                at_ends(lambda d: part_copy(g, d).start())

    def v_copy(g, d):
        return end_copy(v.at[1, g], v.at[2 * (1 - d), g], v_ss.at[d, g], v_rs.at[1 - d, g], d)

    def misfit(g):
        at_ends(
            lambda d: end_copy(
                parts.at[2 * d, g], parts_in.at[d, g], part_ss.at[d, g], part_rs.at[d, g], d
            ).wait_recv()
        )
        scale = std_ref[g * size : (g + 1) * size, :]
        total = parts[1, g] + parts_in[0, g] + parts_in[1, g]
        first = g * size
        innov = owned[first : first + size, :]
        ivar = owned[levels + first : levels + first + size, :]
        v[1, g] = scale * ivar * (scale * total - innov)
        at_ends(lambda d: v_copy(g, d).start())

    def backward(g):
        def add(t, start):
            @pl.loop(0, pairs)
            def _(c):
                at = pl.ds(pl.multiple_of(c * 2 * CHUNK, 2 * CHUNK), 2 * CHUNK)
                value = v[t, g, :, at]
                b = (value[:, None, :] * ytap[t, :, at][None]).reshape(rows, 2 * CHUNK)
                last = value * ylast[t, 0:1, at]
                extra = jnp.concatenate([last, jnp.zeros((grown.shape[0] - rows - size, 2 * CHUNK), F32)], axis=0)
                hi, lo = split(jnp.concatenate([b, extra], axis=0))
                whi, wlo = spreadw[t, 0, at, :], spreadw[t, 1, at, :]
                total = dot(jnp.concatenate([hi, lo, hi], axis=1), jnp.concatenate([whi, whi, wlo], axis=0))
                grown[...] += total

        grown[...] = jnp.zeros_like(grown)
        add(1, True)
        for d in range(2):

            @pl.when(ends[d][1])
            def _(d=d):
                end_copy(v.at[1, g], v.at[2 * d, g], v_ss.at[d, g], v_rs.at[d, g], d).wait_recv()

            add(2 * d, False)
        below = pltpu.roll(grown[0:rows, width : 2 * width], 1, 0)
        first = grown[rows : rows + size, width : 2 * width]
        first = jnp.broadcast_to(first[:, None, :], (size, height, width)).reshape(rows, width)
        row = lax.broadcasted_iota(jnp.int32, (size, height, width), 1).reshape(rows, width)
        x = grown[0:rows, 0:width] + jnp.where(row == 0, first, below)
        field[g] = x
        pack_sides(x, back_out, g)
        for d in range(2):
            side_copy(back_out, back_in, back_ss, back_rs, g, d).start()

    def finish(g):
        side_wait(back_out, back_in, back_ss, back_rs, g)
        x = smooth(field[g], unpack(back_in[0, g], back_in[1, g], rows))
        at = slice(g * size, (g + 1) * size)
        out_ref[at] = control_ref[at] + mask[None] * x.reshape(size, height, width)

    for step in range(GROUPS + 3):
        if step < GROUPS:
            forward(step)
        if step == 1:
            take_observations()
        if 0 <= step - 1 < GROUPS:
            misfit(step - 1)
        if 0 <= step - 2 < GROUPS:
            backward(step - 2)
        if 0 <= step - 4 < GROUPS:
            finish(step - 4)
    finish(GROUPS - 1)

    for g in range(GROUPS):
        for d in range(2):
            side_copy(halo_out, halo_in, halo_ss, halo_rs, g, d).wait_send()
            side_copy(back_out, back_in, back_ss, back_rs, g, d).wait_send()
        at_ends(lambda d: part_copy(g, d).wait_send())
        at_ends(lambda d: v_copy(g, d).wait_send())
    at_ends(lambda d: meta_copy(d).wait_send())

    @pl.loop(1, n_lat)
    def _(d):
        first_copy(d).wait_send()

    @pl.loop(1, n_lon)
    def _(d):
        second_copy(d).wait_send()


def shards(n_lon, n_lat, control, land_mask, std_dev, innovation, inverse_var, *slots_of):
    levels = control.shape[0] * control.shape[1]
    height, width = control.shape[2:]
    slots = slots_of[0].shape[0] * slots_of[0].shape[1]
    chunks = slots // CHUNK
    size = levels // GROUPS
    rows = size * height
    packed = packing(rows)[0]
    grown = -(-(rows + size) // 16) * 16
    deep = 2 * levels // n_lon
    dma = pltpu.SemaphoreType.DMA
    group = dma((2, GROUPS))
    sides = pltpu.VMEM((2, GROUPS, packed, width), F32)

    gradient = pl.pallas_call(
        functools.partial(kernel, n_lon, n_lat),
        out_shape=jax.ShapeDtypeStruct((levels, height, width), F32),
        in_specs=[VMEM] * 10,
        out_specs=VMEM,
        scratch_shapes=[
            pltpu.VMEM((2 * width, 2 * width), BF16),
            sides, sides, sides, sides,
            pltpu.VMEM((rows, 2 * width), BF16),
            pltpu.VMEM((grown, 2 * width), F32),
            pltpu.VMEM((GROUPS, rows, width), F32),
            pltpu.VMEM((3, 8, slots), F32),
            pltpu.VMEM((3, chunks, width, 2 * CHUNK), BF16),
            pltpu.VMEM((3, chunks, height, 2 * CHUNK), F32),
            pltpu.VMEM((3, height, slots), F32),
            pltpu.VMEM((3, 8, slots), F32),
            pltpu.VMEM((3, 2, slots, 2 * width), BF16),
            pltpu.VMEM((3, GROUPS, size, slots), F32),
            pltpu.VMEM((2, GROUPS, size, slots), F32),
            pltpu.VMEM((3, GROUPS, size, slots), F32),
            pltpu.VMEM((n_lat, 2 * levels, width), F32),
            pltpu.VMEM((n_lat, 2 * levels, width), F32),
            pltpu.VMEM((n_lon, n_lat * deep, width), F32),
            pltpu.VMEM((n_lon, n_lat * deep, width), F32),
            pltpu.VMEM((2 * levels, slots), F32),
            group, group, group, group, dma((2,)), dma((2,)), group, group, group, group,
            dma((n_lat,)), dma((n_lat,)), dma((n_lon,)), dma((n_lon,)),
        ],
        compiler_params=pltpu.CompilerParams(
            vmem_limit_bytes=VMEM_LIMIT, collective_id=0, has_side_effects=True
        ),
        name="gradient",
    )(
        control.reshape(levels, height, width), land_mask, std_dev.reshape(levels, 1),
        innovation, inverse_var, *slots_of,
    )
    return gradient.reshape(control.shape)


def solution(mesh):
    tile = P("lat", "lon")
    in_specs = (
        P(None, None, "lat", "lon"), tile, P(),
        P(None, "lat", "lon"), P(None, "lat", "lon"),
        tile, tile, tile, tile, tile,
    )
    body = functools.partial(shards, mesh.shape["lon"], mesh.shape["lat"])
    return jax.shard_map(
        body, mesh=mesh, in_specs=in_specs,
        out_specs=P(None, None, "lat", "lon"), check_vma=False,
    )
```

time: 59.9 us -> 47.3 us (0.79)
  the two profiles are of different devices: /device:TPU:8 before, /device:TPU:1 now
where the time goes in v1:
time: 47.3 us; the launch traced here: 47.1 us
  Pallas kernels  43.4 us (92%)
  local copies, waits for them, and re-layouts  3.68 us (8%)
    pallas_call x1, Pallas kernels, shards(): pl.pallas_call(functools.partial(kernel, n_lon, n_lat), out_shape=jax.Sha...  43.4 us
    unnamed x3, local copies, waits for them, and re-layouts  2.99 us

profile of v1, /device:TPU:1, one launch (start us, length us, event | category | flops | bytes accessed | tf_op | source)
XLA Modules:
  0.0 47.1 jit_solution(222813916064946713)
XLA Ops:
  0.0 0.0 copy-start
  0.0 0.7 %copy-done = f32[2,16]{1,0:T(2,128)S(1)} copy-done((f32[2,16]{1,0:T(2,128)S(1)}, f32[2,16]{1,0:T(2,128)}, u32[]{:S(2)}) %copy-start) | copy-done | bytes 152
  0.7 0.7 %reshape.12.std_ref = f32[32,1]{1,0:T(8,128)} reshape(f32[2,16]{1,0:T(2,128)S(1)} %copy-done) | data formatting | bytes 256 | tf_op jit(solution)/shard_map/reshape | solution.py:515
  1.4 43.4 %gradient.1 = f32[32,64,128]{2,1,0:T(8,128)} custom-call(f32[32,64,128]{2,1,0:T(8,128)} %bitcast.3, s32[64,128]{1,0:T(8,128)} %mask_ref.1, f32[32,1]{1,0:T(8,128)} %reshape.12.std_ref, f32[32,4,128]{2,1,0:T(4,128)} %innov_ref.1, f32[32,4,128]{2,1,0:T(4,128)} %ivar_ref.1, s32[4,128]{1,0:T(4,128)} %row_ref.1, s32[4,128]{1,0:T(4,128)} %col_ref.1, ...), custom_call_target="tpu_custom_call" | custom-call | tf_op jit(solution)/shard_map/gradient/pallas_call | solution.py:482
  44.8 2.3 %copy.13 = f32[2,16,64,128]{3,2,1,0:T(8,128)} copy(f32[2,16,64,128]{3,2,1,0:T(8,128)} %bitcast.2) | data formatting | bytes 2097152
Async XLA Ops:
  0.0 0.7 %copy-start = (f32[2,16]{1,0:T(2,128)S(1)}, f32[2,16]{1,0:T(2,128)}, u32[]{:S(2)}) copy-start(f32[2,16]{1,0:T(2,128)} %param.12) | copy-start | bytes 388

commit v2 on v1

--- a/solution.py
+++ b/solution.py
@@ -15,8 +15,8 @@
 CHUNK = 128
 GROUPS = 4
 PIECE = HALF // 2
-VMEM_LIMIT = 56 * 1024 * 1024
 VMEM = pl.BlockSpec(memory_space=pltpu.VMEM)
+HBM = pl.BlockSpec(memory_space=pltpu.HBM)
 F32, BF16 = jnp.float32, jnp.bfloat16
 
 
@@ -154,14 +154,15 @@
 
 def kernel(
     n_lon, n_lat,
+    control_far, mask_far, std_far, innov_far, ivar_far, row_far, col_far, frow_far, fcol_far, counts_far,
+    out_ref,
     control_ref, mask_ref, std_ref, innov_ref, ivar_ref, row_ref, col_ref, frow_ref, fcol_ref, counts_ref,
-    out_ref,
     filt, halo_out, halo_in, back_out, back_in, ahl, grown, field,
     meta, onehot, weight, ytap, ylast, spreadw,
     parts, parts_in, v,
-    stage, land_a, turned, land_b, owned,
+    turned, land_a, stage, land_b, scales,
     halo_ss, halo_rs, back_ss, back_rs, meta_ss, meta_rs, part_ss, part_rs, v_ss, v_rs,
-    a_ss, a_rs, b_ss, b_rs,
+    a_ss, a_rs, b_ss, b_rs, load_sem, control_sem,
 ):
     levels, height, width = control_ref.shape
     slots = meta.shape[2]
@@ -182,10 +183,19 @@
     def _(d):
         pl.semaphore_signal(barrier, inc=1, device_id={"lon": lon, "lat": lax.rem(lat + d, n_lat)})
 
-    mask = mask_ref[...].astype(F32)
+    far = [innov_far, ivar_far, mask_far, row_far, col_far, frow_far, fcol_far, counts_far, std_far]
+    near = [innov_ref, ivar_ref, mask_ref, row_ref, col_ref, frow_ref, fcol_ref, counts_ref, std_ref]
+    loads = [pltpu.make_async_copy(a, b, load_sem.at[i]) for i, (a, b) in enumerate(zip(far, near))]
+    at_group = [pl.ds(g * size, size) for g in range(GROUPS)]
+    control_loads = [
+        pltpu.make_async_copy(control_far.at[at], control_ref.at[at], control_sem.at[g])
+        for g, at in enumerate(at_group)
+    ]
+    for load in loads[:3] + control_loads + loads[3:]:
+        load.start()
 
     def masked(g):
-        part = control_ref[g * size : (g + 1) * size] * mask[None]
+        part = control_ref[pl.ds(g * size, size)] * mask_ref[...].astype(F32)[None]
         return part.reshape(rows, width)
 
     def side_copy(out, landed, ss, rs, g, d):
@@ -212,34 +222,46 @@
         for d in range(2):
             side_copy(halo_out, halo_in, halo_ss, halo_rs, g, d).start()
 
+    deep = 2 * levels // n_lon
+    loads[0].wait()
+    loads[1].wait()
+    blocks = []
+    for i in range(n_lon):
+        g, place = i * deep // (2 * size), i * deep % (2 * size)
+        source, first = (innov_ref, ivar_ref)[place // size], g * size + place % size
+        blocks.append(jnp.concatenate([source[first : first + deep, p, :] for p in range(n_lat)], axis=0))
+    for q, block in enumerate(swap_blocks(blocks)):
+        turned[q] = block
+
+    loads[2].wait()
+    control_loads[0].wait()
     halo_pack(0)
-    for p in range(n_lat):
-        stage[p, 0:levels] = innov_ref[:, p, :]
-        stage[p, levels : 2 * levels] = ivar_ref[:, p, :]
     pl.semaphore_wait(barrier, n_lon - 1 + n_lat - 1)
-    halo_send(0)
 
     def first_copy(d):
         return pltpu.make_async_remote_copy(
-            src_ref=stage.at[lax.rem(lat + d, n_lat)], dst_ref=land_a.at[lat],
+            src_ref=turned.at[lax.rem(lon + d, n_lon)], dst_ref=land_a.at[lon],
             send_sem=a_ss.at[d], recv_sem=a_rs.at[d],
-            device_id={"lon": lon, "lat": lax.rem(lat + d, n_lat)},
+            device_id={"lon": lax.rem(lon + d, n_lon), "lat": lat},
         )
 
     def first_wait(d):
-        source = lax.rem(lat + n_lat - d, n_lat)
+        source = lax.rem(lon + n_lon - d, n_lon)
         pltpu.make_async_remote_copy(
-            src_ref=stage.at[source], dst_ref=land_a.at[source],
+            src_ref=turned.at[source], dst_ref=land_a.at[source],
             send_sem=a_ss.at[d], recv_sem=a_rs.at[d],
-            device_id={"lon": lon, "lat": source},
+            device_id={"lon": source, "lat": lat},
         ).wait_recv()
 
-    @pl.loop(1, n_lat)
+    @pl.loop(1, n_lon)
     def _(d):
         first_copy(d).start()
 
-    land_a[pl.ds(lat, 1)] = stage[pl.ds(lat, 1)]
-
+    halo_send(0)
+    land_a[pl.ds(lon, 1)] = turned[pl.ds(lon, 1)]
+
+    for load in loads[3:]:
+        load.wait()
     describe(mask_ref, row_ref, col_ref, frow_ref, fcol_ref, counts_ref, meta.at[1])
 
     def end_copy(src, dst, send_sem, recv_sem, d):
@@ -255,9 +277,14 @@
         return end_copy(meta.at[1], meta.at[2 * (1 - d)], meta_ss.at[d], meta_rs.at[1 - d], d)
 
     at_ends(lambda d: meta_copy(d).start())
-    for g in range(1, GROUPS):
+    for load in control_loads[1:]:
+        load.wait()
+
+    @pl.loop(1, GROUPS)
+    def _(g):
         halo_pack(g)
         halo_send(g)
+
 
     for d in range(2):
 
@@ -266,6 +293,10 @@
             meta[2 * d] = jnp.zeros(meta.shape[1:], F32)
             v[2 * d] = jnp.zeros(v.shape[1:], F32)
             parts_in[d] = jnp.zeros(parts_in.shape[1:], F32)
+
+    flat = jnp.concatenate([std_ref[i : i + 1, :] for i in range(std_ref.shape[0])], axis=1)
+    eye = iota((levels, levels), 0) == iota((levels, levels), 1)
+    scales[...] = jnp.sum(jnp.where(eye, flat, 0.0), axis=1, keepdims=True)
 
     k = iota((2 * width, width), 0)
     place = jnp.where(k < width, k, jnp.where(k < width + HALF, k - (width + HALF), k - HALF))
@@ -275,9 +306,9 @@
     filt[:, width : 2 * width] = glo
 
     def tables(t):
-        shift = float((t - 1) * height)
-
-        @pl.loop(0, chunks)
+        shift = jnp.asarray((t - 1) * height, jnp.int32).astype(F32)
+
+        @pl.loop(0, chunks, unroll=4)
         def _(c):
             at = pl.ds(pl.multiple_of(c * CHUNK, CHUNK), CHUNK)
             m = meta[t, :, at]
@@ -306,52 +337,44 @@
 
     tables(1)
 
-    @pl.loop(1, n_lat)
+    @pl.loop(1, n_lon)
     def _(d):
         first_wait(d)
 
-    deep = 2 * levels // n_lon
-    blocks = [land_a[:, i * deep : (i + 1) * deep, :].reshape(n_lat * deep, width) for i in range(n_lon)]
-    for q, block in enumerate(swap_blocks(blocks)):
-        turned[q] = block
-
-    def second_copy(d):
+    for i, block in enumerate(swap_blocks([land_a[t] for t in range(n_lon)])):
+        for p in range(n_lat):
+            stage[p, i * deep : (i + 1) * deep] = block[p * deep : (p + 1) * deep]
+
+    def second_copy(o, d, source, target):
+        at = pl.ds(pl.multiple_of(o * 2 * size, size), 2 * size)
         return pltpu.make_async_remote_copy(
-            src_ref=turned.at[lax.rem(lon + d, n_lon)], dst_ref=land_b.at[lon],
-            send_sem=b_ss.at[d], recv_sem=b_rs.at[d],
-            device_id={"lon": lax.rem(lon + d, n_lon), "lat": lat},
-        )
-
-    def second_wait(d):
-        source = lax.rem(lon + n_lon - d, n_lon)
-        pltpu.make_async_remote_copy(
-            src_ref=turned.at[source], dst_ref=land_b.at[source],
-            send_sem=b_ss.at[d], recv_sem=b_rs.at[d],
-            device_id={"lon": source, "lat": lat},
-        ).wait_recv()
-
-    @pl.loop(1, n_lon)
+            src_ref=stage.at[source, at], dst_ref=land_b.at[target, at],
+            send_sem=b_ss.at[o, d], recv_sem=b_rs.at[o, d],
+            device_id={"lon": lon, "lat": source},
+        )
+
+    def second_send(o, d):
+        return second_copy(o, d, lax.rem(lat + d, n_lat), lat)
+
+    @pl.loop(0, GROUPS)
+    def _(o):
+        @pl.loop(1, n_lat)
+        def _(d):
+            second_send(o, d).start()
+
+    land_b[pl.ds(lat, 1)] = stage[pl.ds(lat, 1)]
+
+    at_ends(lambda d: end_copy(meta.at[1], meta.at[2 * d], meta_ss.at[d], meta_rs.at[d], d).wait_recv())
+
+    @pl.loop(0, 2)
     def _(d):
-        second_copy(d).start()
-
-    land_b[pl.ds(lon, 1)] = turned[pl.ds(lon, 1)]
-
-    for d in range(2):
-
-        @pl.when(ends[d][1])
-        def _(d=d):
-            end_copy(meta.at[1], meta.at[2 * d], meta_ss.at[d], meta_rs.at[d], d).wait_recv()
-
         tables(2 * d)
 
-    def take_observations():
-        @pl.loop(1, n_lon)
+    def take_observations(o):
+        @pl.loop(1, n_lat)
         def _(d):
-            second_wait(d)
-
-        for i, block in enumerate(swap_blocks([land_b[t] for t in range(n_lon)])):
-            for s in range(n_lat):
-                owned[i * deep : (i + 1) * deep, s * width : (s + 1) * width] = block[s * deep : (s + 1) * deep]
+            source = lax.rem(lat + n_lat - d, n_lat)
+            second_copy(o, d, source, source).wait_recv()
 
     def smooth(x, beyond):
         hi, lo = split(jnp.concatenate([x, beyond], axis=1))
@@ -366,17 +389,23 @@
         hi, lo = split(smooth(masked(g), unpack(halo_in[0, g], halo_in[1, g], rows)))
         ahl[:, 0:width] = hi
         ahl[:, width : 2 * width] = lo
-        for t in (0, 2, 1):
-
-            @pl.loop(0, chunks)
+        def gather(t, c):
+            one = onehot[t, c]
+            wide = dot(ahl[...], jnp.concatenate([one, one], axis=0))
+            total = jnp.sum(wide.reshape(size, height, 2 * CHUNK) * weight[t, c][None], axis=1)
+            at = pl.ds(pl.multiple_of(c * CHUNK, CHUNK), CHUNK)
+            parts[t, g, :, at] = total[:, :CHUNK] + total[:, CHUNK:]
+
+        @pl.loop(0, 3)
+        def _(k):
+            t = lax.rem(2 * k, 3)
+
+            @pl.loop(0, chunks, unroll=4)
             def _(c):
-                one = onehot[t, c]
-                wide = dot(ahl[...], jnp.concatenate([one, one], axis=0))
-                total = jnp.sum(wide.reshape(size, height, 2 * CHUNK) * weight[t, c][None], axis=1)
-                at = pl.ds(pl.multiple_of(c * CHUNK, CHUNK), CHUNK)
-                parts[t, g, :, at] = total[:, :CHUNK] + total[:, CHUNK:]
-
-            if t == 2:
+                gather(t, c)
+
+            @pl.when(k == 1)
+            def _():
                 at_ends(lambda d: part_copy(g, d).start())
 
     def v_copy(g, d):
@@ -388,37 +417,38 @@
                 parts.at[2 * d, g], parts_in.at[d, g], part_ss.at[d, g], part_rs.at[d, g], d
             ).wait_recv()
         )
-        scale = std_ref[g * size : (g + 1) * size, :]
+        scale = scales[pl.ds(pl.multiple_of(g * size, size), size), :]
         total = parts[1, g] + parts_in[0, g] + parts_in[1, g]
-        first = g * size
-        innov = owned[first : first + size, :]
-        ivar = owned[levels + first : levels + first + size, :]
+        take_observations(g)
+        innov, ivar = (
+            jnp.concatenate(
+                [land_b[s, pl.ds(pl.multiple_of((2 * g + k) * size, size), size), :] for s in range(n_lat)], axis=1
+            )
+            for k in range(2)
+        )
         v[1, g] = scale * ivar * (scale * total - innov)
         at_ends(lambda d: v_copy(g, d).start())
 
     def backward(g):
-        def add(t, start):
-            @pl.loop(0, pairs)
-            def _(c):
-                at = pl.ds(pl.multiple_of(c * 2 * CHUNK, 2 * CHUNK), 2 * CHUNK)
-                value = v[t, g, :, at]
-                b = (value[:, None, :] * ytap[t, :, at][None]).reshape(rows, 2 * CHUNK)
-                last = value * ylast[t, 0:1, at]
-                extra = jnp.concatenate([last, jnp.zeros((grown.shape[0] - rows - size, 2 * CHUNK), F32)], axis=0)
-                hi, lo = split(jnp.concatenate([b, extra], axis=0))
-                whi, wlo = spreadw[t, 0, at, :], spreadw[t, 1, at, :]
-                total = dot(jnp.concatenate([hi, lo, hi], axis=1), jnp.concatenate([whi, whi, wlo], axis=0))
-                grown[...] += total
-
+        at_ends(
+            lambda d: end_copy(v.at[1, g], v.at[2 * d, g], v_ss.at[d, g], v_rs.at[d, g], d).wait_recv()
+        )
         grown[...] = jnp.zeros_like(grown)
-        add(1, True)
-        for d in range(2):
-
-            @pl.when(ends[d][1])
-            def _(d=d):
-                end_copy(v.at[1, g], v.at[2 * d, g], v_ss.at[d, g], v_rs.at[d, g], d).wait_recv()
-
-            add(2 * d, False)
+
+        @pl.loop(0, 3 * pairs, unroll=6)
+        def _(i):
+            t, c = i // pairs, i % pairs
+            at = pl.ds(pl.multiple_of(c * 2 * CHUNK, 2 * CHUNK), 2 * CHUNK)
+            value = v[t, g, :, at]
+            b = (value[:, None, :] * ytap[t, :, at][None]).reshape(rows, 2 * CHUNK)
+            last = value * ylast[t, 0:1, at]
+            spare = grown.shape[0] - rows - size
+            extra = jnp.concatenate([last, jnp.zeros((spare, 2 * CHUNK), F32)], axis=0) if spare else last
+            hi, lo = split(jnp.concatenate([b, extra], axis=0))
+            whi, wlo = spreadw[t, 0, at, :], spreadw[t, 1, at, :]
+            total = dot(jnp.concatenate([hi, lo, hi], axis=1), jnp.concatenate([whi, whi, wlo], axis=0))
+            grown[...] += total
+
         below = pltpu.roll(grown[0:rows, width : 2 * width], 1, 0)
         first = grown[rows : rows + size, width : 2 * width]
         first = jnp.broadcast_to(first[:, None, :], (size, height, width)).reshape(rows, width)
@@ -432,23 +462,21 @@
     def finish(g):
         side_wait(back_out, back_in, back_ss, back_rs, g)
         x = smooth(field[g], unpack(back_in[0, g], back_in[1, g], rows))
-        at = slice(g * size, (g + 1) * size)
-        out_ref[at] = control_ref[at] + mask[None] * x.reshape(size, height, width)
-
-    for step in range(GROUPS + 3):
-        if step < GROUPS:
-            forward(step)
-        if step == 1:
-            take_observations()
-        if 0 <= step - 1 < GROUPS:
-            misfit(step - 1)
-        if 0 <= step - 2 < GROUPS:
-            backward(step - 2)
-        if 0 <= step - 4 < GROUPS:
-            finish(step - 4)
-    finish(GROUPS - 1)
-
-    for g in range(GROUPS):
+        at = pl.ds(g * size, size)
+        out_ref[at] = mask_ref[...].astype(F32)[None] * x.reshape(size, height, width)
+
+    @pl.loop(0, GROUPS + 2)
+    def _(step):
+        pl.when(step < GROUPS)(lambda: forward(step))
+        pl.when((step >= 1) & (step < GROUPS + 1))(lambda: misfit(step - 1))
+        pl.when(step >= 2)(lambda: backward(step - 2))
+
+    @pl.loop(0, GROUPS)
+    def _(g):
+        finish(g)
+
+    @pl.loop(0, GROUPS)
+    def _(g):
         for d in range(2):
             side_copy(halo_out, halo_in, halo_ss, halo_rs, g, d).wait_send()
             side_copy(back_out, back_in, back_ss, back_rs, g, d).wait_send()
@@ -456,13 +484,15 @@
         at_ends(lambda d: v_copy(g, d).wait_send())
     at_ends(lambda d: meta_copy(d).wait_send())
 
-    @pl.loop(1, n_lat)
+    @pl.loop(1, n_lon)
     def _(d):
         first_copy(d).wait_send()
 
-    @pl.loop(1, n_lon)
-    def _(d):
-        second_copy(d).wait_send()
+    @pl.loop(0, GROUPS)
+    def _(o):
+        @pl.loop(1, n_lat)
+        def _(d):
+            second_send(o, d).wait_send()
 
 
 def shards(n_lon, n_lat, control, land_mask, std_dev, innovation, inverse_var, *slots_of):
@@ -479,12 +509,15 @@
     group = dma((2, GROUPS))
     sides = pltpu.VMEM((2, GROUPS, packed, width), F32)
 
+    inputs = [
+        control.reshape(levels, height, width), land_mask, std_dev, innovation, inverse_var, *slots_of,
+    ]
     gradient = pl.pallas_call(
         functools.partial(kernel, n_lon, n_lat),
         out_shape=jax.ShapeDtypeStruct((levels, height, width), F32),
-        in_specs=[VMEM] * 10,
+        in_specs=[HBM] * 10,
         out_specs=VMEM,
-        scratch_shapes=[
+        scratch_shapes=[pltpu.VMEM(x.shape, x.dtype) for x in inputs] + [
             pltpu.VMEM((2 * width, 2 * width), BF16),
             sides, sides, sides, sides,
             pltpu.VMEM((rows, 2 * width), BF16),
@@ -499,23 +532,21 @@
             pltpu.VMEM((3, GROUPS, size, slots), F32),
             pltpu.VMEM((2, GROUPS, size, slots), F32),
             pltpu.VMEM((3, GROUPS, size, slots), F32),
+            pltpu.VMEM((n_lon, n_lat * deep, width), F32),
+            pltpu.VMEM((n_lon, n_lat * deep, width), F32),
             pltpu.VMEM((n_lat, 2 * levels, width), F32),
             pltpu.VMEM((n_lat, 2 * levels, width), F32),
-            pltpu.VMEM((n_lon, n_lat * deep, width), F32),
-            pltpu.VMEM((n_lon, n_lat * deep, width), F32),
-            pltpu.VMEM((2 * levels, slots), F32),
+            pltpu.VMEM((levels, 1), F32),
             group, group, group, group, dma((2,)), dma((2,)), group, group, group, group,
-            dma((n_lat,)), dma((n_lat,)), dma((n_lon,)), dma((n_lon,)),
+            dma((n_lon,)), dma((n_lon,)), dma((GROUPS, n_lat)), dma((GROUPS, n_lat)),
+            dma((9,)), dma((GROUPS,)),
         ],
         compiler_params=pltpu.CompilerParams(
-            vmem_limit_bytes=VMEM_LIMIT, collective_id=0, has_side_effects=True
+            vmem_limit_bytes=56 << 20, collective_id=0, has_side_effects=True
         ),
         name="gradient",
-    )(
-        control.reshape(levels, height, width), land_mask, std_dev.reshape(levels, 1),
-        innovation, inverse_var, *slots_of,
-    )
-    return gradient.reshape(control.shape)
+    )(*inputs)
+    return control + gradient.reshape(control.shape)
 
 
 def solution(mesh):

time: 47.3 us -> 37 us (0.78)
  Pallas kernels: 43.4 us -> 34.4 us
  local copies, waits for them, and re-layouts: 3.68 us -> 0.01 us
  other arithmetic: 0 us -> 2.38 us
    pallas_call x1, Pallas kernels: 43.4 us -> 34.4 us  [shards(): pl.pallas_call(functools.partial(kernel, n_lon, n_lat), out_shape=jax.Sha...]
    unnamed x3 -> x2, local copies, waits for them, and re-layouts: 2.99 us -> 0.01 us
    add x0 -> x1, other arithmetic: none -> 2.38 us  [shards(): return control + gradient.reshape(control.shape)]
    reshape x1 -> x0, local copies, waits for them, and re-layouts: 0.69 us -> none  [shards(): std_dev.reshape(levels, 1)]
where the time goes in v2:
time: 37 us; the launch traced here: 36.8 us
  Pallas kernels  34.4 us (93%)
  other arithmetic  2.38 us (6%)
    pallas_call x1, Pallas kernels, shards(): pl.pallas_call(functools.partial(kernel, n_lon, n_lat), out_shape=jax.Sha...  34.4 us
    add x1, other arithmetic, shards(): return control + gradient.reshape(control.shape)  2.38 us

profile of v2, /device:TPU:1, one launch (start us, length us, event | category | flops | bytes accessed | tf_op | source)
XLA Modules:
  0.0 36.8 jit_solution(17094907807107431099)
XLA Ops:
  0.0 0.0 copy-start
  0.0 34.4 %gradient.1 = f32[32,64,128]{2,1,0:T(8,128)} custom-call(f32[32,64,128]{2,1,0:T(8,128)} %bitcast.2, s32[64,128]{1,0:T(8,128)} %mask_far.1, f32[2,16]{1,0:T(2,128)} %std_far.1, f32[32,4,128]{2,1,0:T(4,128)} %innov_far.1, f32[32,4,128]{2,1,0:T(4,128)} %ivar_far.1, s32[4,128]{1,0:T(4,128)} %row_far.1, s32[4,128]{1,0:T(4,128)} %col_far.1, f32[4,128]{1,0:T(4,128)} %frow_far.1, ...), custom_call_target="tpu_custom_call" | custom-call | tf_op jit(solution)/shard_map/gradient/pallas_call | solution.py:515
  34.5 0.0 copy-done
  34.5 2.4 %add.3 = f32[2,16,64,128]{3,2,1,0:T(8,128)} add(f32[2,16,64,128]{3,2,1,0:T(8,128)S(1)} %copy-done, f32[2,16,64,128]{3,2,1,0:T(8,128)} %bitcast.3) | non-fusion elementwise | flops 262144 | bytes 3145728 | tf_op jit(solution)/shard_map/add | solution.py:549
Async XLA Ops:
  0.0 34.5 %copy-start = (f32[2,16,64,128]{3,2,1,0:T(8,128)S(1)}, f32[2,16,64,128]{3,2,1,0:T(8,128)}, u32[]{:S(2)}) copy-start(f32[2,16,64,128]{3,2,1,0:T(8,128)} %param.10) | copy-start | bytes 3145732

commit v3 on v2

--- a/solution.py
+++ b/solution.py
@@ -201,14 +201,14 @@
     def side_copy(out, landed, ss, rs, g, d):
         return pltpu.make_async_remote_copy(
             src_ref=out.at[d, g], dst_ref=landed.at[1 - d, g],
-            send_sem=ss.at[d, g], recv_sem=rs.at[1 - d, g], device_id=sides[d],
+            send_sem=ss.at[0], recv_sem=rs.at[1 - d, g], device_id=sides[d],
         )
 
     def side_wait(out, landed, ss, rs, g):
         for d in range(2):
             pltpu.make_async_remote_copy(
                 src_ref=out.at[d, g], dst_ref=landed.at[d, g],
-                send_sem=ss.at[d, g], recv_sem=rs.at[d, g], device_id=sides[d],
+                send_sem=ss.at[0], recv_sem=rs.at[d, g], device_id=sides[d],
             ).wait_recv()
 
     def pack_sides(x, out, g):
@@ -241,17 +241,16 @@
     def first_copy(d):
         return pltpu.make_async_remote_copy(
             src_ref=turned.at[lax.rem(lon + d, n_lon)], dst_ref=land_a.at[lon],
-            send_sem=a_ss.at[d], recv_sem=a_rs.at[d],
+            send_sem=a_ss.at[0], recv_sem=a_rs.at[0],
             device_id={"lon": lax.rem(lon + d, n_lon), "lat": lat},
         )
 
-    def first_wait(d):
-        source = lax.rem(lon + n_lon - d, n_lon)
-        pltpu.make_async_remote_copy(
-            src_ref=turned.at[source], dst_ref=land_a.at[source],
-            send_sem=a_ss.at[d], recv_sem=a_rs.at[d],
-            device_id={"lon": source, "lat": lat},
-        ).wait_recv()
+    def first_all():
+        every = pl.ds(0, n_lon - 1)
+        return pltpu.make_async_remote_copy(
+            src_ref=turned.at[every], dst_ref=land_a.at[every],
+            send_sem=a_ss.at[0], recv_sem=a_rs.at[0], device_id=sides[1],
+        )
 
     @pl.loop(1, n_lon)
     def _(d):
@@ -337,9 +336,7 @@
 
     tables(1)
 
-    @pl.loop(1, n_lon)
-    def _(d):
-        first_wait(d)
+    first_all().wait_recv()
 
     for i, block in enumerate(swap_blocks([land_a[t] for t in range(n_lon)])):
         for p in range(n_lat):
@@ -349,7 +346,7 @@
         at = pl.ds(pl.multiple_of(o * 2 * size, size), 2 * size)
         return pltpu.make_async_remote_copy(
             src_ref=stage.at[source, at], dst_ref=land_b.at[target, at],
-            send_sem=b_ss.at[o, d], recv_sem=b_rs.at[o, d],
+            send_sem=b_ss.at[0], recv_sem=b_rs.at[o],
             device_id={"lon": lon, "lat": source},
         )
 
@@ -371,10 +368,11 @@
         tables(2 * d)
 
     def take_observations(o):
-        @pl.loop(1, n_lat)
-        def _(d):
-            source = lax.rem(lat + n_lat - d, n_lat)
-            second_copy(o, d, source, source).wait_recv()
+        every, at = pl.ds(0, n_lat - 1), pl.ds(pl.multiple_of(o * 2 * size, size), 2 * size)
+        pltpu.make_async_remote_copy(
+            src_ref=stage.at[every, at], dst_ref=land_b.at[every, at],
+            send_sem=b_ss.at[0], recv_sem=b_rs.at[o], device_id=sides[1],
+        ).wait_recv()
 
     def smooth(x, beyond):
         hi, lo = split(jnp.concatenate([x, beyond], axis=1))
@@ -382,7 +380,7 @@
         return wide[:, :width] + wide[:, width:] + dot(lo, filt[:, 0:width])
 
     def part_copy(g, d):
-        return end_copy(parts.at[2 * d, g], parts_in.at[1 - d, g], part_ss.at[d, g], part_rs.at[1 - d, g], d)
+        return end_copy(parts.at[2 * d, g], parts_in.at[1 - d, g], part_ss.at[d], part_rs.at[1 - d, g], d)
 
     def forward(g):
         side_wait(halo_out, halo_in, halo_ss, halo_rs, g)
@@ -409,12 +407,12 @@
                 at_ends(lambda d: part_copy(g, d).start())
 
     def v_copy(g, d):
-        return end_copy(v.at[1, g], v.at[2 * (1 - d), g], v_ss.at[d, g], v_rs.at[1 - d, g], d)
+        return end_copy(v.at[1, g], v.at[2 * (1 - d), g], v_ss.at[d], v_rs.at[1 - d, g], d)
 
     def misfit(g):
         at_ends(
             lambda d: end_copy(
-                parts.at[2 * d, g], parts_in.at[d, g], part_ss.at[d, g], part_rs.at[d, g], d
+                parts.at[2 * d, g], parts_in.at[d, g], part_ss.at[d], part_rs.at[d, g], d
             ).wait_recv()
         )
         scale = scales[pl.ds(pl.multiple_of(g * size, size), size), :]
@@ -431,7 +429,7 @@
 
     def backward(g):
         at_ends(
-            lambda d: end_copy(v.at[1, g], v.at[2 * d, g], v_ss.at[d, g], v_rs.at[d, g], d).wait_recv()
+            lambda d: end_copy(v.at[1, g], v.at[2 * d, g], v_ss.at[d], v_rs.at[d, g], d).wait_recv()
         )
         grown[...] = jnp.zeros_like(grown)
 
@@ -475,24 +473,22 @@
     def _(g):
         finish(g)
 
-    @pl.loop(0, GROUPS)
-    def _(g):
-        for d in range(2):
-            side_copy(halo_out, halo_in, halo_ss, halo_rs, g, d).wait_send()
-            side_copy(back_out, back_in, back_ss, back_rs, g, d).wait_send()
-        at_ends(lambda d: part_copy(g, d).wait_send())
-        at_ends(lambda d: v_copy(g, d).wait_send())
-    at_ends(lambda d: meta_copy(d).wait_send())
-
-    @pl.loop(1, n_lon)
-    def _(d):
-        first_copy(d).wait_send()
-
-    @pl.loop(0, GROUPS)
-    def _(o):
-        @pl.loop(1, n_lat)
-        def _(d):
-            second_send(o, d).wait_send()
+    def all_sent(source, sem):
+        pltpu.make_async_remote_copy(
+            src_ref=source, dst_ref=source, send_sem=sem, recv_sem=sem, device_id=sides[1]
+        ).wait_send()
+
+    all_sent(halo_out, halo_ss.at[0])
+    all_sent(back_out, back_ss.at[0])
+    all_sent(turned.at[pl.ds(0, n_lon - 1)], a_ss.at[0])
+    all_sent(stage.at[pl.ds(0, n_lat - 1)], b_ss.at[0])
+
+    def ends_sent(d):
+        all_sent(parts.at[2 * d], part_ss.at[d])
+        all_sent(v.at[1], v_ss.at[d])
+        meta_copy(d).wait_send()
+
+    at_ends(ends_sent)
 
 
 def shards(n_lon, n_lat, control, land_mask, std_dev, innovation, inverse_var, *slots_of):
@@ -506,7 +502,7 @@
     grown = -(-(rows + size) // 16) * 16
     deep = 2 * levels // n_lon
     dma = pltpu.SemaphoreType.DMA
-    group = dma((2, GROUPS))
+    group, both, one = dma((2, GROUPS)), dma((2,)), dma((1,))
     sides = pltpu.VMEM((2, GROUPS, packed, width), F32)
 
     inputs = [
@@ -514,7 +510,7 @@
     ]
     gradient = pl.pallas_call(
         functools.partial(kernel, n_lon, n_lat),
-        out_shape=jax.ShapeDtypeStruct((levels, height, width), F32),
+        out_shape=pltpu.VMEM((levels, height, width), F32),
         in_specs=[HBM] * 10,
         out_specs=VMEM,
         scratch_shapes=[pltpu.VMEM(x.shape, x.dtype) for x in inputs] + [
@@ -537,8 +533,7 @@
             pltpu.VMEM((n_lat, 2 * levels, width), F32),
             pltpu.VMEM((n_lat, 2 * levels, width), F32),
             pltpu.VMEM((levels, 1), F32),
-            group, group, group, group, dma((2,)), dma((2,)), group, group, group, group,
-            dma((n_lon,)), dma((n_lon,)), dma((GROUPS, n_lat)), dma((GROUPS, n_lat)),
+            one, group, one, group, both, both, both, group, both, group, one, one, one, dma((GROUPS,)),
             dma((9,)), dma((GROUPS,)),
         ],
         compiler_params=pltpu.CompilerParams(

time: 37 us -> 33.9 us (0.916)
  Pallas kernels: 34.4 us -> 32.6 us
  other arithmetic: 2.38 us -> 1.15 us
    pallas_call x1, Pallas kernels: 34.4 us -> 32.6 us  [shards(): pl.pallas_call(functools.partial(kernel, n_lon, n_lat), out_shape=pltpu.V...]
    add x1, other arithmetic: 2.38 us -> 1.15 us  [shards(): return control + gradient.reshape(control.shape)]
where the time goes in v3:
time: 33.9 us; the launch traced here: 33.8 us
  Pallas kernels  32.6 us (96%)
  other arithmetic  1.15 us (3%)
    pallas_call x1, Pallas kernels, shards(): pl.pallas_call(functools.partial(kernel, n_lon, n_lat), out_shape=pltpu.V...  32.6 us
    add x1, other arithmetic, shards(): return control + gradient.reshape(control.shape)  1.15 us

profile of v3, /device:TPU:1, one launch (start us, length us, event | category | flops | bytes accessed | tf_op | source)
XLA Modules:
  0.0 33.8 jit_solution(4440474666950911120)
XLA Ops:
  0.0 0.0 copy-start
  0.0 32.6 %gradient.1 = f32[32,64,128]{2,1,0:T(8,128)S(1)} custom-call(f32[32,64,128]{2,1,0:T(8,128)} %bitcast.3, s32[64,128]{1,0:T(8,128)} %mask_far.1, f32[2,16]{1,0:T(2,128)} %std_far.1, f32[32,4,128]{2,1,0:T(4,128)} %innov_far.1, f32[32,4,128]{2,1,0:T(4,128)} %ivar_far.1, s32[4,128]{1,0:T(4,128)} %row_far.1, s32[4,128]{1,0:T(4,128)} %col_far.1, ...), custom_call_target="tpu_custom_call" | custom-call | tf_op jit(solution)/shard_map/gradient/pallas_call | solution.py:511
  32.6 0.0 copy-done
  32.6 1.2 %add.3 = f32[2,16,64,128]{3,2,1,0:T(8,128)} add(f32[2,16,64,128]{3,2,1,0:T(8,128)S(1)} %copy-done, f32[2,16,64,128]{3,2,1,0:T(8,128)S(1)} %bitcast.2) | non-fusion elementwise | flops 262144 | bytes 3145728 | tf_op jit(solution)/shard_map/add | solution.py:544
Async XLA Ops:
  0.0 32.6 %copy-start = (f32[2,16,64,128]{3,2,1,0:T(8,128)S(1)}, f32[2,16,64,128]{3,2,1,0:T(8,128)}, u32[]{:S(2)}) copy-start(f32[2,16,64,128]{3,2,1,0:T(8,128)} %param.10) | copy-start | bytes 3145732

commit v4 on v3

--- a/solution.py
+++ b/solution.py
@@ -236,6 +236,10 @@
     loads[2].wait()
     control_loads[0].wait()
     halo_pack(0)
+    for load in loads[3:]:
+        load.wait()
+    describe(mask_ref, row_ref, col_ref, frow_ref, fcol_ref, counts_ref, meta.at[1])
+
     pl.semaphore_wait(barrier, n_lon - 1 + n_lat - 1)
 
     def first_copy(d):
@@ -257,12 +261,6 @@
         first_copy(d).start()
 
     halo_send(0)
-    land_a[pl.ds(lon, 1)] = turned[pl.ds(lon, 1)]
-
-    for load in loads[3:]:
-        load.wait()
-    describe(mask_ref, row_ref, col_ref, frow_ref, fcol_ref, counts_ref, meta.at[1])
-
     def end_copy(src, dst, send_sem, recv_sem, d):
         return pltpu.make_async_remote_copy(
             src_ref=src, dst_ref=dst, send_sem=send_sem, recv_sem=recv_sem, device_id=ends[d][0]
@@ -283,7 +281,6 @@
     def _(g):
         halo_pack(g)
         halo_send(g)
-
 
     for d in range(2):
 
@@ -336,6 +333,9 @@
 
     tables(1)
 
+    land_a[pl.ds(lon, 1)] = turned[pl.ds(lon, 1)]
+
+
     first_all().wait_recv()
 
     for i, block in enumerate(swap_blocks([land_a[t] for t in range(n_lon)])):
@@ -394,7 +394,7 @@
             at = pl.ds(pl.multiple_of(c * CHUNK, CHUNK), CHUNK)
             parts[t, g, :, at] = total[:, :CHUNK] + total[:, CHUNK:]
 
-        @pl.loop(0, 3)
+        @pl.loop(0, 3, unroll=3)
         def _(k):
             t = lax.rem(2 * k, 3)
 

time: 33.9 us -> 33.2 us (0.979)
  Pallas kernels: 32.6 us -> 31.9 us
    pallas_call x1, Pallas kernels: 32.6 us -> 31.9 us  [shards(): pl.pallas_call(functools.partial(kernel, n_lon, n_lat), out_shape=pltpu.V...]
where the time goes in v4:
time: 33.2 us; the launch traced here: 33 us
  Pallas kernels  31.9 us (96%)
  other arithmetic  1.15 us (3%)
    pallas_call x1, Pallas kernels, shards(): pl.pallas_call(functools.partial(kernel, n_lon, n_lat), out_shape=pltpu.V...  31.9 us
    add x1, other arithmetic, shards(): return control + gradient.reshape(control.shape)  1.15 us

profile of v4, /device:TPU:1, one launch (start us, length us, event | category | flops | bytes accessed | tf_op | source)
XLA Modules:
  0.0 33.0 jit_solution(4533646509513527937)
XLA Ops:
  0.0 0.0 copy-start
  0.0 31.9 %gradient.1 = f32[32,64,128]{2,1,0:T(8,128)S(1)} custom-call(f32[32,64,128]{2,1,0:T(8,128)} %bitcast.3, s32[64,128]{1,0:T(8,128)} %mask_far.1, f32[2,16]{1,0:T(2,128)} %std_far.1, f32[32,4,128]{2,1,0:T(4,128)} %innov_far.1, f32[32,4,128]{2,1,0:T(4,128)} %ivar_far.1, s32[4,128]{1,0:T(4,128)} %row_far.1, s32[4,128]{1,0:T(4,128)} %col_far.1, ...), custom_call_target="tpu_custom_call" | custom-call | tf_op jit(solution)/shard_map/gradient/pallas_call | solution.py:511
  31.9 0.0 copy-done
  31.9 1.2 %add.3 = f32[2,16,64,128]{3,2,1,0:T(8,128)} add(f32[2,16,64,128]{3,2,1,0:T(8,128)S(1)} %copy-done, f32[2,16,64,128]{3,2,1,0:T(8,128)S(1)} %bitcast.2) | non-fusion elementwise | flops 262144 | bytes 3145728 | tf_op jit(solution)/shard_map/add | solution.py:544
Async XLA Ops:
  0.0 31.9 %copy-start = (f32[2,16,64,128]{3,2,1,0:T(8,128)S(1)}, f32[2,16,64,128]{3,2,1,0:T(8,128)}, u32[]{:S(2)}) copy-start(f32[2,16,64,128]{3,2,1,0:T(8,128)} %param.10) | copy-start | bytes 3145732

commit v5 on v4

--- a/solution.py
+++ b/solution.py
@@ -175,11 +175,11 @@
 
     barrier = pltpu.get_barrier_semaphore()
 
-    @pl.loop(1, n_lon)
+    @pl.loop(1, n_lon, unroll=min(7, n_lon - 1))
     def _(d):
         pl.semaphore_signal(barrier, inc=1, device_id={"lon": lax.rem(lon + d, n_lon), "lat": lat})
 
-    @pl.loop(1, n_lat)
+    @pl.loop(1, n_lat, unroll=min(3, n_lat - 1))
     def _(d):
         pl.semaphore_signal(barrier, inc=1, device_id={"lon": lon, "lat": lax.rem(lat + d, n_lat)})
 
@@ -218,9 +218,16 @@
     def halo_pack(g):
         pack_sides(masked(g), halo_out, g)
 
+    def side_send(out, landed, ss, rs, g):
+        for k in range(2):
+            d = lax.rem(lon + k, 2)
+            pltpu.make_async_remote_copy(
+                src_ref=out.at[d, g], dst_ref=landed.at[1 - d, g], send_sem=ss.at[0], recv_sem=rs.at[1 - d, g],
+                device_id={"lon": lax.rem(lon + n_lon - 1 + 2 * d, n_lon), "lat": lat},
+            ).start()
+
     def halo_send(g):
-        for d in range(2):
-            side_copy(halo_out, halo_in, halo_ss, halo_rs, g, d).start()
+        side_send(halo_out, halo_in, halo_ss, halo_rs, g)
 
     deep = 2 * levels // n_lon
     loads[0].wait()
@@ -256,7 +263,7 @@
             send_sem=a_ss.at[0], recv_sem=a_rs.at[0], device_id=sides[1],
         )
 
-    @pl.loop(1, n_lon)
+    @pl.loop(1, n_lon, unroll=min(7, n_lon - 1))
     def _(d):
         first_copy(d).start()
 
@@ -355,7 +362,7 @@
 
     @pl.loop(0, GROUPS)
     def _(o):
-        @pl.loop(1, n_lat)
+        @pl.loop(1, n_lat, unroll=min(3, n_lat - 1))
         def _(d):
             second_send(o, d).start()
 
@@ -454,14 +461,13 @@
         x = grown[0:rows, 0:width] + jnp.where(row == 0, first, below)
         field[g] = x
         pack_sides(x, back_out, g)
-        for d in range(2):
-            side_copy(back_out, back_in, back_ss, back_rs, g, d).start()
+        side_send(back_out, back_in, back_ss, back_rs, g)
 
     def finish(g):
         side_wait(back_out, back_in, back_ss, back_rs, g)
         x = smooth(field[g], unpack(back_in[0, g], back_in[1, g], rows))
         at = pl.ds(g * size, size)
-        out_ref[at] = mask_ref[...].astype(F32)[None] * x.reshape(size, height, width)
+        out_ref[at] = control_ref[at] + mask_ref[...].astype(F32)[None] * x.reshape(size, height, width)
 
     @pl.loop(0, GROUPS + 2)
     def _(step):
@@ -541,7 +547,7 @@
         ),
         name="gradient",
     )(*inputs)
-    return control + gradient.reshape(control.shape)
+    return gradient.reshape(control.shape)
 
 
 def solution(mesh):

time: 33.2 us -> 33 us (level)
  other arithmetic: 1.15 us -> 0 us
  local copies, waits for them, and re-layouts: 0.01 us -> 0.97 us
    add x1 -> x0, other arithmetic: 1.15 us -> none  [shards(): return control + gradient.reshape(control.shape)]
    unnamed x2 -> x1, local copies, waits for them, and re-layouts: 0.01 us -> 0.97 us
where the time goes in v5:
time: 33 us; the launch traced here: 32.8 us
  Pallas kernels  31.8 us (96%)
  local copies, waits for them, and re-layouts  0.97 us (3%)
    pallas_call x1, Pallas kernels, shards(): pl.pallas_call(functools.partial(kernel, n_lon, n_lat), out_shape=pltpu.V...  31.8 us
    unnamed x1, local copies, waits for them, and re-layouts  0.97 us

profile of v5, /device:TPU:1, one launch (start us, length us, event | category | flops | bytes accessed | tf_op | source)
XLA Modules:
  0.0 32.8 jit_solution(10270654412144845613)
XLA Ops:
  0.0 31.8 %gradient.1 = f32[32,64,128]{2,1,0:T(8,128)S(1)} custom-call(f32[32,64,128]{2,1,0:T(8,128)} %bitcast.3, s32[64,128]{1,0:T(8,128)} %mask_far.1, f32[2,16]{1,0:T(2,128)} %std_far.1, f32[32,4,128]{2,1,0:T(4,128)} %innov_far.1, f32[32,4,128]{2,1,0:T(4,128)} %ivar_far.1, s32[4,128]{1,0:T(4,128)} %row_far.1, s32[4,128]{1,0:T(4,128)} %col_far.1, ...), custom_call_target="tpu_custom_call" | custom-call | tf_op jit(solution)/shard_map/gradient/pallas_call | solution.py:517
  31.8 1.0 %copy.12 = f32[2,16,64,128]{3,2,1,0:T(8,128)} copy(f32[2,16,64,128]{3,2,1,0:T(8,128)S(1)} %bitcast.2) | data formatting | bytes 2097152
